TPU v7x, 32 devices: a whole 2x2x4 slice. The times are simulated.
32 devices in a mesh: coil: 2 (over x), slab: 16 (over z, y, core).
Axes of the slice: x: 2, y: 2, z: 4, core: 2. Of those that a mesh axis runs over, the one named last changes fastest.
Arguments:
- solution: float32 [2, 1, 128, 192, 256], P(None, None, 'slab', 'coil'), may hold values from -6 to 6
- residual: float32 [2, 1, 128, 192, 256], P(None, None, 'slab', 'coil'), may hold values from -6 to 6
- direction: float32 [2, 1, 128, 192, 256], P(None, None, 'slab', 'coil'), may hold values from -6 to 6
- sens_maps: float32 [2, 16, 128, 192, 256], P(None, 'coil', 'slab'), may hold values from -1.05 to 1.05
- sampling: int32 [1, 128, 192], replicated, may hold values from 0 to 1, as said below
Outputs:
- next_solution: float32 [2, 1, 128, 192, 256], P(None, None, 'slab', 'coil')
- next_residual: float32 [2, 1, 128, 192, 256], P(None, None, 'slab', 'coil')
- next_direction: float32 [2, 1, 128, 192, 256], P(None, None, 'slab', 'coil')
Inputs may be any that keep to these rules, and one draw needn't show every extreme that they name: sampling is 1 on every line whose kx lies within 4 of 0 or of 128 and whose ky lies within 4 of 0 or of 192.
All inputs are finite; a program needn't handle non-finite values.
Results may differ from a plain program's by a relative error of at most 0.00016.
Values sent between devices are 32-bit elements; how exact they have to be, the bound alone decides.
A program may use at most 192 MiB of HBM per device.

v0:
```python
import math

import jax
import jax.numpy as jnp
from jax import lax
from jax.sharding import PartitionSpec as P

damping_weight = 0.5


def dft_table(length, inverse):
    index = jnp.arange(length, dtype=jnp.int32)
    phase = (index[:, None] * index[None, :] % length).astype(jnp.float32)
    angle = phase * (2.0 * math.pi / length)
    scale = 1.0 / math.sqrt(length)
    cosine = jnp.cos(angle) * scale
    sine = jnp.sin(angle) * scale
    if inverse:
        return jnp.stack([jnp.stack([cosine, -sine]), jnp.stack([sine, cosine])])
    return jnp.stack([jnp.stack([cosine, sine]), jnp.stack([-sine, cosine])])


def front_second(table, data):
    return jnp.einsum(
        "abky,wbcfxy->wacfxk",
        table,
        data,
        precision=lax.Precision.HIGHEST,
        preferred_element_type=jnp.float32,
    )


def front_first(table, data):
    return jnp.einsum(
        "abkx,wbcfxy->wacfky",
        table,
        data,
        precision=lax.Precision.HIGHEST,
        preferred_element_type=jnp.float32,
    )


def front_product(maps, field):
    real_part = (
        maps[:, 0][:, :, None] * field[:, 0][:, None]
        - maps[:, 1][:, :, None] * field[:, 1][:, None]
    )
    imag_part = (
        maps[:, 0][:, :, None] * field[:, 1][:, None]
        + maps[:, 1][:, :, None] * field[:, 0][:, None]
    )
    return jnp.stack([real_part, imag_part], axis=1)


def front_combine(maps, data):
    real_part = jnp.sum(
        maps[:, 0][:, :, None] * data[:, 0] + maps[:, 1][:, :, None] * data[:, 1], axis=1
    )
    imag_part = jnp.sum(
        maps[:, 0][:, :, None] * data[:, 1] - maps[:, 1][:, :, None] * data[:, 0], axis=1
    )
    return jnp.stack([real_part, imag_part], axis=1)


def front_mask(table_fwd, table_inv, weight, data):
    spectra = front_first(table_fwd, data)
    return front_first(table_inv, spectra * weight)


def readout_front(data, groups):
    shape = data.shape
    split = data.reshape(shape[:-1] + (groups, shape[-1] // groups))
    count = len(shape)
    return jnp.transpose(split, (count - 1, count) + tuple(range(count - 1)))


def readout_back(data):
    count = data.ndim
    moved = jnp.transpose(data, tuple(range(2, count)) + (0, 1))
    shape = moved.shape
    return moved.reshape(shape[:-2] + (shape[-2] * shape[-1],))


def body(solution, residual, direction, sens_maps, sampling):
    size_x = sampling.shape[1]
    size_y = sampling.shape[2]
    groups = lax.axis_size("slab")
    first_fwd = dft_table(size_x, False)
    first_inv = dft_table(size_x, True)
    second_fwd = dft_table(size_y, False)
    second_inv = dft_table(size_y, True)
    weight = sampling.astype(jnp.float32)[None, None, None, :, :, :]
    moved_dir, moved_maps = (
        lax.all_to_all(
            readout_front(direction, groups), "slab", split_axis=0, concat_axis=4, tiled=True
        ),
        lax.all_to_all(
            readout_front(sens_maps, groups), "slab", split_axis=0, concat_axis=4, tiled=True
        ),
    )
    full_dir = lax.all_gather(moved_dir[0], "coil", axis=4, tiled=True)
    maps_here = moved_maps[0]
    coil_data = front_second(second_fwd, front_product(maps_here, full_dir))
    masked = front_mask(first_fwd, first_inv, weight, coil_data)
    partial_value = front_combine(maps_here, front_second(second_inv, masked))
    shared = lax.psum_scatter(partial_value, "coil", scatter_dimension=4, tiled=True)
    combined = readout_back(
        lax.all_to_all(shared[None], "slab", split_axis=4, concat_axis=0, tiled=True)
    )
    image_ap = combined + damping_weight * direction
    norm_now = lax.psum(jnp.sum(residual * residual), ("coil", "slab"))
    curvature = lax.psum(jnp.sum(direction * image_ap), ("coil", "slab"))
    alpha = norm_now / curvature
    next_residual = residual - alpha * image_ap
    fresh = lax.psum(jnp.sum(next_residual * next_residual), ("coil", "slab"))
    next_solution = solution + alpha * direction
    next_direction = next_residual + fresh / norm_now * direction
    return (next_solution, next_residual, next_direction)


def solution(mesh):
    in_specs = (
        P(None, None, "slab", "coil", None),
        P(None, None, "slab", "coil", None),
        P(None, None, "slab", "coil", None),
        P(None, "coil", "slab", None, None),
        P(),
    )
    out_specs = (
        P(None, None, "slab", "coil", None),
        P(None, None, "slab", "coil", None),
        P(None, None, "slab", "coil", None),
    )
    return jax.shard_map(body, mesh=mesh, in_specs=in_specs, out_specs=out_specs, check_vma=False)
```

profile of v0, /device:TPU:0, one launch (start us, length us, event | category | flops | bytes accessed | tf_op | source)
XLA Modules:
  0.0 1277.4 jit_solution(8715549475650694544)
XLA Ops:
  7.2 1.8 copy.53
  9.0 0.0 copy-start
  9.0 1.9 copy.39
  10.9 0.2 copy-done
  11.0 7.4 all-to-all-start.1
  18.5 28.8 %copy.34 = f32[2,8,8,192,256]{3,4,2,1,0:T(8,128)} copy(f32[2,8,8,192,256]{4,3,2,1,0:T(8,128)} %param.8) | data formatting | bytes 50331648 | tf_op args[3]
  47.3 23.7 %copy.35 = f32[16,16,2,8,8,192]{5,1,4,3,2,0:T(8,128)} copy(f32[16,16,2,8,8,192]{5,1,0,4,3,2:T(8,128)} %bitcast.178) | data formatting | bytes 50331648 | tf_op jit(solution)/shard_map/transpose | solution.py:74
  71.0 0.0 all-to-all-done.1
  71.0 6.0 all-to-all-start
  77.0 0.0 all-gather.2.cloned.1.call-start
  77.0 2.3 copy.80
  79.3 1.8 copy.41
  81.1 0.0 all-gather.2.cloned.1.call-update
  81.1 0.3 reduce-scatter.2.cloned.1.call-start
  81.5 0.3 fusion.47
  81.7 0.3 sine_multiply_fusion.1
  82.0 0.8 fusion.40
  82.8 0.8 sine_multiply_fusion
  83.6 0.7 fusion.39
  84.3 1.2 fusion.26
  85.6 0.0 copy-done.10
  85.6 41.9 %all-gather.2.cloned.1.call-done = f32[16,2,1,128,192]{3,0,2,1,4:T(8,128)} async-done(((f32[16,2,1,128,96]{3,0,2,1,4:T(8,128)}), f32[16,2,1,128,192]{3,0,2,1,4:T(8,128)}) %all-gather.2.cloned.1.call-update) | async-done | bytes 3145744 | tf_op jit(solution)/shard_map/all_gather | solution.py:101
  127.5 2.1 slice_bitcast_fusion.3
  129.6 0.5 copy.42
  130.1 0.5 copy.44
  130.6 535.2 %all-to-all-done = f32[16,16,2,8,8,192]{5,1,4,3,2,0:T(8,128)} async-done(((f32[16,16,2,8,8,192]{5,1,4,3,2,0:T(8,128)}), f32[16,16,2,8,8,192]{5,1,4,3,2,0:T(8,128)}, u32[]{:S(2)}, u32[]{:S(2)}) %all-to-all-start) | async-done | bytes 25165856 | tf_op jit(solution)/shard_map/all_to_all | solution.py:97
  665.9 30.8 %copy.78 = f32[1,16,2,8,16,8,192]{6,5,4,3,2,1,0:T(8,128)} copy(f32[1,16,2,8,16,8,192]{6,1,5,3,2,4,0:T(8,128)} %bitcast.3) | data formatting | bytes 50331648 | tf_op jit(solution)/shard_map/all_to_all | solution.py:97
  696.7 21.4 %fusion.52 = (f32[16,1,8,128,192]{4,3,2,1,0:T(8,128)}, f32[16,1,8,128,192]{4,3,2,1,0:T(8,128)}) fusion(f32[16,2,8,128,192]{4,3,2,1,0:T(8,128)} %bitcast.179), kind=kLoop, calls=%fused_computation.97 | loop fusion | bytes 50331648 | tf_op jit(solution)/shard_map/slice | solution.py:57
  718.0 16.2 %copy.73 = f32[16,1,8,128,192]{3,4,2,0,1:T(8,128)} copy(f32[16,1,8,128,192]{4,3,2,1,0:T(8,128)} %get-tuple-element.15) | data formatting | bytes 25165824
  734.2 16.2 %copy.74 = f32[16,1,8,128,192]{3,4,2,0,1:T(8,128)} copy(f32[16,1,8,128,192]{4,3,2,1,0:T(8,128)} %get-tuple-element.16) | data formatting | bytes 25165824
  750.4 15.6 %fusion.9 = (f32[16,1,8,1,128,192]{4,5,1,2,0,3:T(8,128)S(1)}, f32[16,1,8,1,128,192]{4,5,1,2,0,3:T(8,128)}) fusion(f32[16,1,8,128,192]{3,4,2,0,1:T(8,128)} %copy.74, f32[16,1,8,128,192]{3,4,2,0,1:T(8,128)} %copy.73, f32[16,128,192]{1,2,0:T(8,128)S(1)} %copy.44, f32[16,128,192]{1,2,0:T(8,128)S(1)} %copy.42), kind=kLoop, calls=%fused_computation.16 | loop fusion | flops 18874368 | bytes 53477376 | tf_op jit(solution)/shard_map/sub | solution.py:45
  766.0 0.0 copy-done.6
  766.0 0.0 copy-start.9
  766.0 47.1 %fusion = f32[16,8,128,2,192,1]{2,4,5,3,1,0:T(8,128)} fusion(f32[16,1,8,1,128,192]{4,5,1,2,0,3:T(8,128)} %get-tuple-element.18, f32[16,1,8,1,128,192]{4,5,1,2,0,3:T(8,128)S(1)} %get-tuple-element.17, f32[1,2,192,192]{3,2,1,0:T(8,128)S(1)} %copy-done.6, f32[1,2,192,192]{3,2,1,0:T(8,128)S(1)} %copy-done.7), kind=kOutput, calls=%fused_computation.2 | convolution fusion | flops 28997468160 | bytes 50921472 | tf_op jit(solution)/shard_map/abky,wbcfxy->wacfxk/dot_general | solution.py:24
  813.1 0.0 copy-done.9
  813.1 24.7 %fusion.7 = f32[16,8,192,2,128,1]{4,2,5,3,1,0:T(8,128)S(1)} fusion(f32[16,8,128,2,192,1]{2,4,5,3,1,0:T(8,128)} %fusion, f32[1,2,128,128]{3,2,1,0:T(8,128)S(1)} %copy-done.8, f32[1,2,128,128]{3,2,1,0:T(8,128)S(1)} %copy-done.9), kind=kOutput, calls=%fused_computation.10 | convolution fusion | flops 19327418368 | bytes 50593792 | tf_op jit(solution)/shard_map/abkx,wbcfxy->wacfky/dot_general | solution.py:34
  837.8 0.0 copy-start.4
  837.9 0.0 slice-start
  837.9 0.0 slice-start.1
  837.9 23.2 %fusion.5 = f32[16,8,192,2,128,1]{4,2,5,3,1,0:T(8,128)} fusion(f32[16,8,192,2,128,1]{4,2,5,3,1,0:T(8,128)S(1)} %fusion.7, f32[128,192]{0,1:T(8,128)S(1)} %convert_bitcast_fusion, f32[1,2,128,128]{3,2,1,0:T(8,128)S(1)} %get-tuple-element.34, f32[1,2,128,128]{3,2,1,0:T(8,128)S(1)} %get-tuple-element.29), kind=kOutput, calls=%fused_computation.7 | convolution fusion | flops 19333709824 | bytes 50692096 | tf_op jit(solution)/shard_map/abkx,wbcfxy->wacfky/dot_general | solution.py:34
  861.1 47.8 %fusion.16 = f32[16,2,8,1,128,192]{4,5,2,0,3,1:T(8,128)} fusion(f32[16,8,192,2,128,1]{4,2,5,3,1,0:T(8,128)} %fusion.5, f32[1,2,192,192]{3,2,1,0:T(8,128)S(1)} %copy-done.5, f32[1,2,192,192]{3,2,1,0:T(8,128)S(1)} %copy-done.4), kind=kOutput, calls=%fused_computation.29 | convolution fusion | flops 28991176704 | bytes 50921472 | tf_op jit(solution)/shard_map/abky,wbcfxy->wacfxk/dot_general | solution.py:24
  908.9 15.9 %fusion.12 = (f32[16,128,192]{1,2,0:T(8,128)S(1)}, f32[16,128,192]{1,2,0:T(8,128)}) fusion(f32[16,1,8,128,192]{3,4,2,0,1:T(8,128)} %copy.74, f32[16,1,8,128,192]{3,4,2,0,1:T(8,128)S(1)} %bitcast.181, f32[16,2,8,1,128,192]{4,5,2,0,3,1:T(8,128)} %fusion.16), kind=kLoop, calls=%fused_computation.21 | loop fusion | flops 24379392 | bytes 53477376 | tf_op jit(solution)/shard_map/reduce_sum | solution.py:56
  924.8 1.7 pad_maximum_fusion
  926.5 3.5 copy.48
  930.0 0.0 reduce-scatter.2.cloned.1.call-update
  930.0 176.4 %reduce-scatter.2.cloned.1.call-done = f32[16,2,1,128,96]{3,0,2,1,4:T(8,128)} async-done(((f32[16,2,1,128,192]{3,0,2,1,4:T(8,128)}), f32[16,2,1,128,96]{3,0,2,1,4:T(8,128)}) %reduce-scatter.2.cloned.1.call-update) | async-done | bytes 1572880 | tf_op jit(solution)/shard_map/reduce_scatter | solution.py:106
  1106.4 3.2 copy.49
  1109.6 5.6 all-to-all-start.2
  1115.3 2.8 copy.56
  1118.1 2.4 multiply_reduce_fusion.2
  1120.5 35.9 %all-to-all-done.2 = f32[1,16,2,1,128,96]{5,2,1,3,0,4:T(2,128)S(1)} async-done(((f32[1,16,2,1,128,96]{5,2,1,3,0,4:T(2,128)}), f32[1,16,2,1,128,96]{5,2,1,3,0,4:T(2,128)S(1)}, u32[]{:S(2)}, u32[]{:S(2)}) %all-to-all-start.2) | async-done | bytes 1572896 | tf_op jit(solution)/shard_map/all_to_all | solution.py:108
  1156.4 1.2 copy.79
  1157.6 1.2 copy.51
  1158.8 0.0 copy-start.2
  1158.8 1.3 copy-done.2
  1160.2 1.1 multiply_reduce_fusion.1
  1161.3 2.8 copy.55
  1164.1 46.5 %all-reduce = (f32[]{:T(128)}, f32[]{:T(128)}) all-reduce(f32[]{:T(128)} %multiply_reduce_fusion.2, f32[]{:T(128)} %multiply_reduce_fusion.1), channel_id=1, replica_groups=mesh['coil'=2,'slab'=16] {'coil','slab'}, use_global_device_ids=true, to_apply=%region_1.2 | all-reduce | flops 2 | bytes 16 | tf_op jit(solution)/shard_map/psum | solution.py:111
  1212.0 4.7 multiply_reduce_fusion
  1216.7 39.9 %psum.23 = f32[]{:T(128)} all-reduce(f32[]{:T(128)} %get-tuple-element.13), channel_id=1, replica_groups=mesh['coil'=2,'slab'=16] {'coil','slab'}, use_global_device_ids=true, to_apply=%region_8.9 | all-reduce | flops 1 | bytes 8 | tf_op jit(solution)/shard_map/psum | solution.py:115
  1257.9 2.8 copy.59
  1260.7 4.8 multiply_add_fusion
  1265.5 2.9 copy.58
  1268.4 1.7 copy.60
  (19 shorter events, 0.0 us)
Async XLA Ops:
  9.0 2.0 copy-start
  11.0 59.9 %all-to-all-start.1 = ((f32[16,16,2,1,8,96]{5,1,4,2,3,0:T(8,128)}), f32[16,16,2,1,8,96]{5,1,4,2,3,0:T(8,128)}, u32[]{:S(2)}, u32[]{:S(2)}) async-start(f32[16,16,2,1,8,96]{5,1,4,2,3,0:T(8,128)} %copy.39), calls=%async_computation.1 | async-start | bytes 4194304 | tf_op jit(solution)/shard_map/all_to_all | solution.py:94
  71.0 594.9 %all-to-all-start = ((f32[16,16,2,8,8,192]{5,1,4,3,2,0:T(8,128)}), f32[16,16,2,8,8,192]{5,1,4,3,2,0:T(8,128)}, u32[]{:S(2)}, u32[]{:S(2)}) async-start(f32[16,16,2,8,8,192]{5,1,4,3,2,0:T(8,128)} %copy.35), calls=%async_computation | async-start | bytes 67108864 | tf_op jit(solution)/shard_map/all_to_all | solution.py:97
  77.0 50.5 %all-gather.2.cloned.1.call-start = ((), (), s32[]{:S(2)}) async-start(), calls=%async_computation.4 | async-start | bytes 4718592 | tf_op jit(solution)/shard_map/all_gather | solution.py:101
  81.1 4.5 copy-start.10
  81.1 1025.3 %reduce-scatter.2.cloned.1.call-start = ((), (), s32[]{:S(2)}) async-start(), calls=%async_computation.5 | async-start | bytes 4718592 | tf_op jit(solution)/shard_map/reduce_scatter | solution.py:106
  750.4 15.6 %copy-start.6 = (f32[1,2,192,192]{3,2,1,0:T(8,128)S(1)}, f32[1,2,192,192]{3,2,1,0:T(8,128)}, u32[]{:S(2)}) copy-start(f32[1,2,192,192]{3,2,1,0:T(8,128)} %get-tuple-element.24) | copy-start | bytes 884740
  750.4 15.6 %copy-start.7 = (f32[1,2,192,192]{3,2,1,0:T(8,128)S(1)}, f32[1,2,192,192]{3,2,1,0:T(8,128)}, u32[]{:S(2)}) copy-start(f32[1,2,192,192]{3,2,1,0:T(8,128)} %get-tuple-element.27) | copy-start | bytes 884740
  766.0 47.1 %copy-start.8 = (f32[1,2,128,128]{3,2,1,0:T(8,128)S(1)}, f32[1,2,128,128]{3,2,1,0:T(8,128)}, u32[]{:S(2)}) copy-start(f32[1,2,128,128]{3,2,1,0:T(8,128)} %get-tuple-element.30) | copy-start | bytes 393220
  766.0 47.1 %copy-start.9 = (f32[1,2,128,128]{3,2,1,0:T(8,128)S(1)}, f32[1,2,128,128]{3,2,1,0:T(8,128)}, u32[]{:S(2)}) copy-start(f32[1,2,128,128]{3,2,1,0:T(8,128)} %get-tuple-element.33) | copy-start | bytes 393220
  837.8 23.3 %copy-start.4 = (f32[1,2,192,192]{3,2,1,0:T(8,128)S(1)}, f32[1,2,192,192]{3,2,1,0:T(8,128)}, u32[]{:S(2)}) copy-start(f32[1,2,192,192]{3,2,1,0:T(8,128)} %get-tuple-element.23) | copy-start | bytes 884740
  837.8 23.3 %copy-start.5 = (f32[1,2,192,192]{3,2,1,0:T(8,128)S(1)}, f32[1,2,192,192]{3,2,1,0:T(8,128)}, u32[]{:S(2)}) copy-start(f32[1,2,192,192]{3,2,1,0:T(8,128)} %get-tuple-element.28) | copy-start | bytes 884740
  837.9 71.0 %slice-start = ((s8[12582912]{0:T(1024)(128)(4,1)}), s8[4194304]{0:T(1024)(128)(4,1)S(1)}, s32[]{:S(2)}) async-start(s8[12582912]{0:T(1024)(128)(4,1)} %bitcast.180), calls=%async_computation.6 | async-start | bytes 8388608
  837.9 71.0 %slice-start.1 = ((s8[12582912]{0:T(1024)(128)(4,1)}), s8[4194304]{0:T(1024)(128)(4,1)S(1)}, s32[]{:S(2)}) async-start(s8[12582912]{0:T(1024)(128)(4,1)} %bitcast.180), calls=%async_computation.7 | async-start | bytes 8388608
  861.1 47.8 %slice-start.2 = ((s8[12582912]{0:T(1024)(128)(4,1)}), s8[4194304]{0:T(1024)(128)(4,1)S(1)}, s32[]{:S(2)}) async-start(s8[12582912]{0:T(1024)(128)(4,1)} %bitcast.180), calls=%async_computation.8 | async-start | bytes 8388608
  1109.6 46.7 %all-to-all-start.2 = ((f32[1,16,2,1,128,96]{5,2,1,3,0,4:T(2,128)}), f32[1,16,2,1,128,96]{5,2,1,3,0,4:T(2,128)S(1)}, u32[]{:S(2)}, u32[]{:S(2)}) async-start(f32[1,16,2,1,128,96]{5,2,1,3,0,4:T(2,128)} %copy.49), calls=%async_computation.3 | async-start | bytes 4194304 | tf_op jit(solution)/shard_map/all_to_all | solution.py:108
  1157.6 2.6 copy-start.1
  1158.8 1.3 copy-start.2
  1265.5 2.9 copy-start.3
Sparse Core Ops, SparseCore 0:
  81.2 46.1 all-gather.1
  930.2 176.2 reduce-scatter.1
where the time goes:
time: 1280 us
  waiting for transfers between devices  789 us (62%)
  local copies, waits for them, and re-layouts  172 us (13%)
  matrix products  143 us (11%)
  blocking collectives  86.4 us (7%)
  other arithmetic  50.3 us (4%)
  starting transfers between devices  19.4 us (2%)
  between operations  17.3 us (1%)
    all_to_all x1, waiting for transfers between devices, body(): lax.all_to_all(readout_front(sens_maps, groups), 'slab', split_axis=0, co...  535 us
    reduce_scatter x1, waiting for transfers between devices, body(): lax.psum_scatter(partial_value, 'coil', scatter_dimension=4, tiled=True)  176 us
    dot_general x2, matrix products, front_second(): jnp.einsum('abky,wbcfxy->wacfxk', table, data, precision=lax.Precision.HI...  94.8 us
    unnamed x37, local copies, waits for them, and re-layouts  77.6 us
    dot_general x2, matrix products, front_first(): jnp.einsum('abkx,wbcfxy->wacfky', table, data, precision=lax.Precision.HI...  48 us
    psum x1, blocking collectives, body(): norm_now = lax.psum(jnp.sum(residual * residual), ('coil', 'slab'))  46.5 us
    all_gather x1, waiting for transfers between devices, body(): full_dir = lax.all_gather(moved_dir[0], 'coil', axis=4, tiled=True)  41.9 us
    psum x1, blocking collectives, body(): fresh = lax.psum(jnp.sum(next_residual * next_residual), ('coil', 'slab'))  39.9 us
  transfers between devices with their start and end apart: 5, of which 4 were waited for; matrix products, arithmetic and copies ran while one was open for 5% of the time, Pallas kernels for 0%

commit v1 on v0

v1 whole, which is shorter than its diff:
```python
import math

import jax
import jax.numpy as jnp
import numpy as np
from jax import lax
from jax.experimental.layout import Layout, with_layout_constraint
from jax.sharding import PartitionSpec as P

damping_weight = 0.5
lanes = 128


def dft_table(length, inverse):
    index = np.arange(length)
    angle = (index[:, None] * index[None, :] % length) * (2.0 * math.pi / length)
    scale = 1.0 / math.sqrt(length)
    cosine = np.cos(angle) * scale
    sine = np.sin(angle) * scale
    if inverse:
        table = np.stack([np.stack([cosine, -sine]), np.stack([sine, cosine])])
    else:
        table = np.stack([np.stack([cosine, sine]), np.stack([-sine, cosine])])
    return jnp.asarray(table.astype(np.float32))


def second_pass(table, data):
    return jnp.einsum(
        "abky,wbcxy->wacxk",
        table,
        data,
        precision=lax.Precision.HIGH,
        preferred_element_type=jnp.float32,
    )


def first_pass(table, data):
    return jnp.einsum(
        "abkx,wbcxy->wacky",
        table,
        data,
        precision=lax.Precision.HIGH,
        preferred_element_type=jnp.float32,
    )


def row_major(data):
    return with_layout_constraint(data, Layout(major_to_minor=tuple(range(data.ndim))))


def pack(maps, groups):
    _, coils, rows, size_y, size_z = maps.shape
    split = maps.reshape(2, coils, rows, size_y, groups, size_z // groups)
    moved = jnp.transpose(split, (4, 0, 1, 2, 5, 3))
    whole = size_y // lanes * lanes
    if size_y - whole != lanes // 2:
        return moved
    tails = jnp.concatenate([moved[:, 0, ..., whole:], moved[:, 1, ..., whole:]], axis=-1)
    pieces = []
    for start in range(0, whole, lanes):
        pieces.append(moved[:, :, ..., start : start + lanes])
    return jnp.concatenate(pieces + [tails[:, None]], axis=1)


def unpack(data, size_y):
    groups, _, coils, rows, depth, _ = data.shape
    whole = size_y // lanes * lanes
    parts = []
    for part in range(2):
        if size_y - whole != lanes // 2:
            value = data[:, part]
        else:
            tail = data[:, -1, ..., part * (lanes // 2) : (part + 1) * (lanes // 2)]
            heads = [data[:, 2 * step + part] for step in range(whole // lanes)]
            value = jnp.concatenate(heads + [tail], axis=-1)
        moved = jnp.transpose(value, (3, 1, 0, 2, 4))
        parts.append(moved.reshape(depth, coils, groups * rows, size_y))
    return parts


def body(solution, residual, direction, sens_maps, sampling):
    size_x, size_y = sampling.shape[1:]
    size_z = direction.shape[-1]
    rows = direction.shape[2]
    coils = sens_maps.shape[1]
    groups = lax.axis_size("slab")
    members = lax.axis_size("coil")
    width = size_y // members
    everyone = groups * members
    first_fwd = dft_table(size_x, False)
    first_inv = dft_table(size_x, True)
    second_fwd = dft_table(size_y, False)
    second_inv = dft_table(size_y, True)
    weight = sampling[0].astype(jnp.float32)
    spans = 2 if size_z // groups >= 16 else 1
    depth = size_z // spans // groups

    moved = direction[:, 0].reshape(2, rows, width, spans, groups, depth)
    moved = jnp.transpose(moved, (4, 3, 0, 1, 5, 2))
    moved = lax.all_to_all(moved, "slab", split_axis=0, concat_axis=0, tiled=True)
    moved = lax.all_gather(moved, "coil", axis=5, tiled=True)
    moved = jnp.transpose(moved, (1, 4, 2, 0, 3, 5))
    fields = moved.reshape(spans, depth, 2, size_x, size_y)

    def apply(maps, field):
        real_map, imag_map = maps
        real_in = field[:, 0][:, None]
        imag_in = field[:, 1][:, None]
        data = jnp.stack(
            [real_map * real_in - imag_map * imag_in, real_map * imag_in + imag_map * real_in], axis=1
        )
        spectra = first_pass(first_fwd, second_pass(second_fwd, data)) * weight
        data = second_pass(second_inv, first_pass(first_inv, spectra))
        real_out = jnp.sum(real_map * data[:, 0] + imag_map * data[:, 1], axis=1)
        imag_out = jnp.sum(real_map * data[:, 1] - imag_map * data[:, 0], axis=1)
        return jnp.stack([real_out, imag_out], axis=1)

    combined = []
    for span in range(spans):
        extent = size_z // spans
        here = sens_maps[..., span * extent : (span + 1) * extent]
        half, quarter = coils // 2, coils // 4
        cuts = (0, half, half + quarter, coils) if span == spans - 1 else (0, half, coils)
        total = None
        for low, high in zip(cuts[:-1], cuts[1:]):
            sent = row_major(pack(here[:, low:high], groups))
            landed = lax.all_to_all(sent, "slab", split_axis=0, concat_axis=0, tiled=True)
            value = apply(unpack(landed, size_y), fields[span])
            total = value if total is None else total + value
        parts = total.reshape(depth, 2, size_x, members, width)
        parts = jnp.transpose(parts, (3, 2, 1, 0, 4))
        parts = lax.all_to_all(parts, "coil", split_axis=0, concat_axis=0, tiled=True)
        summed = jnp.sum(parts, axis=0).reshape(groups, rows, 2, depth, width)
        back = lax.all_to_all(summed, "slab", split_axis=0, concat_axis=0, tiled=True)
        combined.append(jnp.transpose(back, (2, 1, 4, 0, 3)).reshape(2, 1, rows, width, extent))
    image_ap = row_major(jnp.concatenate(combined, axis=-1)) + damping_weight * direction

    sums = jnp.stack(
        [
            jnp.sum(residual * residual),
            jnp.sum(direction * image_ap),
            jnp.sum(residual * image_ap),
            jnp.sum(image_ap * image_ap),
        ]
    )
    sums = jnp.broadcast_to(jnp.pad(sums, (0, lanes - 4)), (everyone, 1, lanes))
    sums = lax.all_to_all(sums, ("coil", "slab"), split_axis=0, concat_axis=0, tiled=True)
    sums = jnp.sum(sums, axis=(0, 1))
    norm_now, curvature, cross, square = sums[0], sums[1], sums[2], sums[3]
    alpha = norm_now / curvature
    fresh = norm_now - 2.0 * alpha * cross + alpha * alpha * square
    next_residual = residual - alpha * image_ap
    next_solution = solution + alpha * direction
    next_direction = next_residual + fresh / norm_now * direction
    return (next_solution, next_residual, next_direction)


def solution(mesh):
    field = P(None, None, "slab", "coil", None)
    in_specs = (field, field, field, P(None, "coil", "slab", None, None), P())
    out_specs = (field, field, field)
    return jax.shard_map(body, mesh=mesh, in_specs=in_specs, out_specs=out_specs, check_vma=False)
```

time: 1280 us -> 1190 us (0.930)
  waiting for transfers between devices: 789 us -> 517 us
  local copies, waits for them, and re-layouts: 172 us -> 336 us
  starting transfers between devices: 19.4 us -> 105 us
  matrix products: 143 us -> 67.1 us
  blocking collectives: 86.4 us -> 12.8 us
  other arithmetic: 50.3 us -> 118 us
    all_to_all x3 -> x10, waiting for transfers between devices: 571 us -> 262 us  [the longest x5 175 us: body(): lax.all_to_all(sent, 'slab', split_axis=0, concat_axis=0, tiled=True)]
    all_gather x1, waiting for transfers between devices: 41.9 us -> 255 us  [body(): moved = lax.all_gather(moved, 'coil', axis=5, tiled=True)]
    reduce_scatter x1 -> x0, waiting for transfers between devices: 176 us -> none  [body(): lax.psum_scatter(partial_value, 'coil', scatter_dimension=4, tiled=True)]
    slice x1 -> x21, local copies, waits for them, and re-layouts: 21.4 us -> 114 us  [the longest x15 52.3 us: apply(): real_out = jnp.sum(real_map * data[:, 0] + imag_map * data[:, 1], axis=1)]
    psum x2 -> x0, blocking collectives: 86.4 us -> none  [the longest x1 46.5 us: body(): norm_now = lax.psum(jnp.sum(residual * residual), ('coil', 'slab'))]
    all_to_all x3 -> x10, starting transfers between devices: 19.1 us -> 105 us  [the longest x5 76.1 us: body(): lax.all_to_all(sent, 'slab', split_axis=0, concat_axis=0, tiled=True)]
    dot_general x4 -> x20, matrix products: 143 us -> 67.1 us  [the longest x10 45.1 us: second_pass(): jnp.einsum('abky,wbcxy->wacxk', table, data, precision=lax.Precision.HIGH...]
    reshape x0 -> x14, local copies, waits for them, and re-layouts: none -> 47 us  [the longest x10 41.6 us: unpack(): parts.append(moved.reshape(depth, coils, groups * rows, size_y))]
  transfers between devices with their start and end apart: 5 -> 11, of which waited for: 4 -> 8; matrix products, arithmetic and copies ran while one was open for 5% -> 43% of each run, Pallas kernels for 0% -> 0%
where the time goes in v1:
time: 1190 us; the launch traced here: 1170 us
  waiting for transfers between devices  517 us (43%)
  local copies, waits for them, and re-layouts  336 us (28%)
  other arithmetic  118 us (10%)
  starting transfers between devices  105 us (9%)
  matrix products  67.1 us (6%)
  between operations  19.1 us (2%)
  blocking collectives  12.8 us (1%)
    all_gather x1, waiting for transfers between devices, body(): moved = lax.all_gather(moved, 'coil', axis=5, tiled=True)  255 us
    all_to_all x5, waiting for transfers between devices, body(): lax.all_to_all(sent, 'slab', split_axis=0, concat_axis=0, tiled=True)  175 us
    all_to_all x5, starting transfers between devices, body(): lax.all_to_all(sent, 'slab', split_axis=0, concat_axis=0, tiled=True)  76.1 us
    slice x15, local copies, waits for them, and re-layouts, apply(): real_out = jnp.sum(real_map * data[:, 0] + imag_map * data[:, 1], axis=1)  52.3 us
    reduce_sum x5, other arithmetic, apply(): real_out = jnp.sum(real_map * data[:, 0] + imag_map * data[:, 1], axis=1)  48.3 us
    dot_general x10, matrix products, second_pass(): jnp.einsum('abky,wbcxy->wacxk', table, data, precision=lax.Precision.HIGH...  45.1 us
    all_to_all x2, waiting for transfers between devices, body(): lax.all_to_all(summed, 'slab', split_axis=0, concat_axis=0, tiled=True)  42.7 us
    slice x3, local copies, waits for them, and re-layouts, body(): value = apply(unpack(landed, size_y), fields[span])  42.1 us
  transfers between devices with their start and end apart: 11, of which 8 were waited for; matrix products, arithmetic and copies ran while one was open for 43% of the time, Pallas kernels for 0%

profile of v1, /device:TPU:0, one launch (start us, length us, event | category | flops | bytes accessed | tf_op | source)
XLA Modules:
  0.0 1174.8 jit_solution(17411200076861966679)
XLA Ops:
  10.7 7.4 all-to-all-start.1
  18.1 5.1 fusion.74
  32.0 27.3 %all-to-all-done.1 = f32[16,2,2,8,8,96]{5,4,1,3,2,0:T(8,128)} async-done(((f32[16,2,2,8,8,96]{5,4,1,3,2,0:T(8,128)}), f32[16,2,2,8,8,96]{5,4,1,3,2,0:T(8,128)}, u32[]{:S(2)}, u32[]{:S(2)}) %all-to-all-start.1) | async-done | bytes 1572896 | tf_op jit(solution)/shard_map/all_to_all | solution.py:100
  59.3 11.2 all-to-all-start.6
  70.5 5.0 copy.521
  80.9 49.0 %all-to-all-done.6 = f32[16,3,2,8,8,128]{5,4,3,2,1,0:T(8,128)S(1)} async-done(((f32[16,3,2,8,8,128]{5,4,3,2,1,0:T(8,128)}), f32[16,3,2,8,8,128]{5,4,3,2,1,0:T(8,128)S(1)}, u32[]{:S(2)}, u32[]{:S(2)}) %all-to-all-start.6) | async-done | bytes 3145760 | tf_op jit(solution)/shard_map/all_to_all | solution.py:127
  129.9 15.5 %all-to-all-start.7 = ((f32[16,3,2,8,8,128]{5,4,3,2,1,0:T(8,128)}), f32[16,3,2,8,8,128]{5,4,3,2,1,0:T(8,128)}, u32[]{:S(2)}, u32[]{:S(2)}) async-start(f32[16,3,2,8,8,128]{5,4,3,2,1,0:T(8,128)} %pad_maximum_fusion.4), calls=%async_computation.7 | async-start | bytes 6291456 | tf_op jit(solution)/shard_map/all_to_all | solution.py:127
  145.3 13.7 %fusion.72 = (f32[2,4,8,192,128]{4,3,2,1,0:T(8,128)}, f32[2,4,8,192,128]{4,3,2,1,0:T(8,128)}, f32[2,4,8,192,128]{4,3,2,1,0:T(8,128)}) fusion(f32[2,8,8,192,256]{4,3,2,1,0:T(8,128)} %param.12), kind=kLoop, calls=%fused_computation.184 | loop fusion | bytes 37748736 | tf_op jit(solution)/shard_map/slice | solution.py:126
  159.0 8.2 copy.515
  176.0 28.8 %all-to-all-done.7 = f32[16,3,2,8,8,128]{5,4,3,2,1,0:T(8,128)} async-done(((f32[16,3,2,8,8,128]{5,4,3,2,1,0:T(8,128)}), f32[16,3,2,8,8,128]{5,4,3,2,1,0:T(8,128)}, u32[]{:S(2)}, u32[]{:S(2)}) %all-to-all-start.7) | async-done | bytes 3145760 | tf_op jit(solution)/shard_map/all_to_all | solution.py:127
  204.8 15.5 %all-to-all-start.5 = ((f32[16,3,4,8,8,128]{5,4,3,2,1,0:T(8,128)}), f32[16,3,4,8,8,128]{5,4,3,2,1,0:T(8,128)}, u32[]{:S(2)}, u32[]{:S(2)}) async-start(f32[16,3,4,8,8,128]{5,4,3,2,1,0:T(8,128)} %pad_maximum_fusion.2), calls=%async_computation.5 | async-start | bytes 12582912 | tf_op jit(solution)/shard_map/all_to_all | solution.py:127
  220.2 8.2 copy.512
  228.4 4.4 copy_bitcast_fusion.1
  237.3 97.1 %all-to-all-done.5 = f32[16,3,4,8,8,128]{5,4,3,2,1,0:T(8,128)} async-done(((f32[16,3,4,8,8,128]{5,4,3,2,1,0:T(8,128)}), f32[16,3,4,8,8,128]{5,4,3,2,1,0:T(8,128)}, u32[]{:S(2)}, u32[]{:S(2)}) %all-to-all-start.5) | async-done | bytes 6291488 | tf_op jit(solution)/shard_map/all_to_all | solution.py:127
  334.4 28.1 %all-to-all-start.2 = ((f32[16,3,4,8,8,128]{5,4,3,2,1,0:T(8,128)}), f32[16,3,4,8,8,128]{5,4,3,2,1,0:T(8,128)}, u32[]{:S(2)}, u32[]{:S(2)}) async-start(f32[16,3,4,8,8,128]{5,4,3,2,1,0:T(8,128)} %pad_maximum_fusion.1), calls=%async_computation.2 | async-start | bytes 12582912 | tf_op jit(solution)/shard_map/all_to_all | solution.py:127
  363.1 8.2 copy.509
  371.3 9.3 copy.339
  380.6 4.4 copy_bitcast_fusion.2
  386.4 4.7 pad_maximum_fusion
  421.2 254.5 %all-gather.2.cloned.1.call-done = f32[16,2,2,8,8,192]{0,4,3,2,1,5:T(8,128)} async-done(((f32[16,2,2,8,8,96]{0,4,3,2,1,5:T(8,128)}), f32[16,2,2,8,8,192]{0,4,3,2,1,5:T(8,128)}) %all-gather.2.cloned.1.call-update) | async-done | bytes 3145744 | tf_op jit(solution)/shard_map/all_gather | solution.py:101
  675.7 19.3 %fusion.73 = (f32[1,8,2,16,8,192]{3,1,4,2,0,5:T(8,128)}, f32[1,8,2,16,8,192]{3,1,4,2,0,5:T(8,128)}) fusion(f32[2,8,2,16,8,192]{3,1,4,2,0,5:T(8,128)} %bitcast.553), kind=kLoop, calls=%fused_computation.185 | loop fusion | bytes 6291456 | tf_op jit(solution)/shard_map/slice | solution.py:128
  695.0 11.9 %copy.340 = f32[1,8,2,16,8,192]{5,4,3,2,1,0:T(8,128)} copy(f32[1,8,2,16,8,192]{3,1,4,2,0,5:T(8,128)} %get-tuple-element.22) | data formatting | bytes 3145728 | tf_op jit(solution)/shard_map/slice | solution.py:128
  707.0 10.9 copy.385
  720.6 5.9 all-to-all-start
  734.1 6.1 multiply_subtract_fusion.5
  756.9 7.8 add_reduce_fusion.4
  770.4 4.6 fusion.30
  788.7 7.8 add_reduce_fusion.3
  804.9 4.5 slice_bitcast_fusion.8
  816.0 5.3 copy.362
  821.3 5.6 copy.586
  826.9 5.2 copy.364
  834.7 4.5 slice_bitcast_fusion.2
  845.9 5.2 copy.387
  851.1 5.6 copy.584
  856.7 5.7 copy.390
  866.7 5.3 fusion.6
  877.3 5.4 fusion.54
  885.8 4.9 copy.393
  890.7 4.9 copy.395
  895.6 12.8 %add_reduce_fusion = (f32[8,16,8,192]{3,0,2,1:T(8,128)}, f32[8,16,8,192]{3,0,2,1:T(8,128)S(1)}) fusion(f32[8,4,16,8,192]{4,3,2,1,0:T(8,128)} %bitcast.565, f32[8,4,16,8,192]{4,3,2,1,0:T(8,128)} %bitcast.564, f32[16,4,8,8,64]{4,3,2,1,0:T(8,128)} %copy-done.18, f32[16,4,8,8,128]{4,3,2,1,0:T(8,128)} %copy-done.16, f32[16,4,8,8,64]{4,3,2,1,0:T(8,128)} %copy-done.17, ...), kind=kLoop, calls=%fused_computation.54 | loop fusion | flops 7471104 | bytes 14155776 | tf_op jit(solution)/shard_map/reduce_sum | solution.py:114
  913.0 6.0 fusion.57
  923.0 4.6 all-to-all-start.8
  930.2 4.5 slice_bitcast_fusion.14
  941.3 5.2 copy.342
  946.5 5.5 copy.588
  952.0 5.3 copy.345
  957.3 6.1 multiply_subtract_fusion.2
  963.5 5.3 fusion.3
  974.1 5.4 fusion.51
  979.5 5.3 fusion
  990.3 5.3 fusion.48
  1000.8 5.0 copy.367
  1009.3 4.9 copy.369
  1014.2 5.1 copy.350
  1019.4 13.0 %add_reduce_fusion.1 = (f32[8,16,8,192]{3,0,2,1:T(8,128)}, f32[8,16,8,192]{3,0,2,1:T(8,128)S(1)}) fusion(f32[8,4,16,8,192]{4,3,2,1,0:T(8,128)} %bitcast.563, f32[8,4,16,8,192]{4,3,2,1,0:T(8,128)} %bitcast.562, f32[16,4,8,8,64]{4,3,2,1,0:T(8,128)} %copy-done.6, f32[16,4,8,8,128]{4,3,2,1,0:T(8,128)} %copy-done.4, f32[16,4,8,8,64]{4,3,2,1,0:T(8,128)} %copy-done.5, ...), kind=kLoop, calls=%fused_computation.56 | loop fusion | flops 7471104 | bytes 14155776 | tf_op jit(solution)/shard_map/reduce_sum | solution.py:114
  1032.5 6.9 add_reduce_fusion.2
  1060.0 17.2 %all-to-all-done.3 = f32[2,128,2,8,96]{1,4,3,2,0:T(8,128)S(1)} async-done(((f32[2,128,2,8,96]{1,4,3,2,0:T(8,128)}), f32[2,128,2,8,96]{1,4,3,2,0:T(8,128)S(1)}, u32[]{:S(2)}, u32[]{:S(2)}) %all-to-all-start.3) | async-done | bytes 1572896 | tf_op jit(solution)/shard_map/all_to_all | solution.py:132
  1077.2 5.8 all-to-all-start.9
  1084.5 21.4 %all-to-all-done.9 = f32[16,8,2,8,96]{4,3,2,1,0:T(8,128)S(1)} async-done(((f32[16,8,2,8,96]{4,3,2,1,0:T(8,128)}), f32[16,8,2,8,96]{4,3,2,1,0:T(8,128)S(1)}, u32[]{:S(2)}, u32[]{:S(2)}) %all-to-all-start.9) | async-done | bytes 786464 | tf_op jit(solution)/shard_map/all_to_all | solution.py:134
  1106.8 6.9 all-to-all-start.4
  1115.4 21.3 %all-to-all-done.4 = f32[16,8,2,8,96]{4,3,2,1,0:T(8,128)} async-done(((f32[16,8,2,8,96]{4,3,2,1,0:T(8,128)}), f32[16,8,2,8,96]{4,3,2,1,0:T(8,128)}, u32[]{:S(2)}, u32[]{:S(2)}) %all-to-all-start.4) | async-done | bytes 786464 | tf_op jit(solution)/shard_map/all_to_all | solution.py:134
  1145.9 12.8 %all_to_all.55 = f32[32,1,128]{2,1,0:T(1,128)S(1)} all-to-all(f32[32,1,128]{2,1,0:T(1,128)S(1)} %broadcast_in_dim.28), channel_id=1, replica_groups=mesh['coil'=2,'slab'=16] {'coil','slab'}, dimensions={0} | all-to-all | bytes 32768 | tf_op jit(solution)/shard_map/all_to_all | solution.py:147
  1163.2 4.5 multiply_add_fusion.3
  (196 shorter events, 217.7 us)
Async XLA Ops:
  10.7 48.6 %all-to-all-start.1 = ((f32[16,2,2,8,8,96]{5,4,1,3,2,0:T(8,128)}), f32[16,2,2,8,8,96]{5,4,1,3,2,0:T(8,128)}, u32[]{:S(2)}, u32[]{:S(2)}) async-start(f32[16,2,2,8,8,96]{5,4,1,3,2,0:T(8,128)} %copy.338), calls=%async_computation.1 | async-start | bytes 4194304 | tf_op jit(solution)/shard_map/all_to_all | solution.py:100
  59.3 70.6 %all-to-all-start.6 = ((f32[16,3,2,8,8,128]{5,4,3,2,1,0:T(8,128)}), f32[16,3,2,8,8,128]{5,4,3,2,1,0:T(8,128)S(1)}, u32[]{:S(2)}, u32[]{:S(2)}) async-start(f32[16,3,2,8,8,128]{5,4,3,2,1,0:T(8,128)} %pad_maximum_fusion.3), calls=%async_computation.6 | async-start | bytes 6291456 | tf_op jit(solution)/shard_map/all_to_all | solution.py:127
  129.9 74.9 %all-to-all-start.7 = ((f32[16,3,2,8,8,128]{5,4,3,2,1,0:T(8,128)}), f32[16,3,2,8,8,128]{5,4,3,2,1,0:T(8,128)}, u32[]{:S(2)}, u32[]{:S(2)}) async-start(f32[16,3,2,8,8,128]{5,4,3,2,1,0:T(8,128)} %pad_maximum_fusion.4), calls=%async_computation.7 | async-start | bytes 6291456 | tf_op jit(solution)/shard_map/all_to_all | solution.py:127
  204.8 129.7 %all-to-all-start.5 = ((f32[16,3,4,8,8,128]{5,4,3,2,1,0:T(8,128)}), f32[16,3,4,8,8,128]{5,4,3,2,1,0:T(8,128)}, u32[]{:S(2)}, u32[]{:S(2)}) async-start(f32[16,3,4,8,8,128]{5,4,3,2,1,0:T(8,128)} %pad_maximum_fusion.2), calls=%async_computation.5 | async-start | bytes 12582912 | tf_op jit(solution)/shard_map/all_to_all | solution.py:127
  334.4 386.2 %all-to-all-start.2 = ((f32[16,3,4,8,8,128]{5,4,3,2,1,0:T(8,128)}), f32[16,3,4,8,8,128]{5,4,3,2,1,0:T(8,128)}, u32[]{:S(2)}, u32[]{:S(2)}) async-start(f32[16,3,4,8,8,128]{5,4,3,2,1,0:T(8,128)} %pad_maximum_fusion.1), calls=%async_computation.2 | async-start | bytes 12582912 | tf_op jit(solution)/shard_map/all_to_all | solution.py:127
  362.6 313.2 %all-gather.2.cloned.1.call-start = ((), (), s32[]{:S(2)}) async-start(), calls=%async_computation.11 | async-start | bytes 37748736 | tf_op jit(solution)/shard_map/all_gather | solution.py:101
  385.5 0.9 copy-start.44
  393.5 5.5 copy-start.22
  393.5 5.5 copy-start.24
  397.0 2.1 copy-start.25
  397.0 2.8 copy-start.26
  411.9 2.6 copy-start.27
  411.9 2.6 copy-start.29
  412.3 2.2 copy-start.30
  412.3 2.3 copy-start.31
  720.6 202.3 %all-to-all-start = ((f32[16,3,4,8,8,128]{5,4,3,2,1,0:T(8,128)}), f32[16,3,4,8,8,128]{5,4,3,2,1,0:T(8,128)}, u32[]{:S(2)}, u32[]{:S(2)}) async-start(f32[16,3,4,8,8,128]{5,4,3,2,1,0:T(8,128)} %pad_maximum_fusion), calls=%async_computation | async-start | bytes 12582912 | tf_op jit(solution)/shard_map/all_to_all | solution.py:127
  728.1 3.8 copy-start.41
  732.2 8.0 copy-start.32
  734.1 6.2 copy-start.34
  734.1 6.1 copy-start.1
  740.2 2.8 copy-start.37
  743.0 1.5 copy-start.36
  744.5 1.5 copy-start
  750.7 6.1 copy-start.28
  782.9 5.7 copy-start.23
  804.8 4.5 copy-start.2
  804.8 4.5 copy-start.4
  809.3 3.4 copy-start.5
  809.4 3.3 copy-start.6
  834.7 4.5 copy-start.15
  834.7 4.5 copy-start.16
  839.2 3.4 copy-start.17
  839.2 3.3 copy-start.18
  856.7 5.7 copy-start.33
  856.7 5.8 copy-start.35
  866.7 5.3 copy-start.38
  923.0 130.2 %all-to-all-start.8 = ((f32[2,128,2,8,96]{1,4,3,2,0:T(8,128)}), f32[2,128,2,8,96]{1,4,3,2,0:T(8,128)}, u32[]{:S(2)}, u32[]{:S(2)}) async-start(f32[2,128,2,8,96]{1,4,3,2,0:T(8,128)} %copy.441), calls=%async_computation.8 | async-start | bytes 3145728 | tf_op jit(solution)/shard_map/all_to_all | solution.py:132
  930.1 4.5 copy-start.7
  930.1 4.5 copy-start.9
  934.7 3.4 copy-start.11
  934.7 3.3 copy-start.13
  952.0 5.3 copy-start.43
  1014.2 5.1 copy-start.3
  1019.4 13.0 %copy-start.8 = (f32[16,4,8,8,128]{4,3,2,1,0:T(8,128)S(1)}, f32[16,4,8,8,128]{4,3,2,1,0:T(8,128)}, u32[]{:S(2)}) copy-start(f32[16,4,8,8,128]{4,3,2,1,0:T(8,128)} %copy-done.7) | copy-start | bytes 6291460
  1019.4 13.0 %copy-start.10 = (f32[16,4,8,8,128]{4,3,2,1,0:T(8,128)S(1)}, f32[16,4,8,8,128]{4,3,2,1,0:T(8,128)}, u32[]{:S(2)}) copy-start(f32[16,4,8,8,128]{4,3,2,1,0:T(8,128)} %copy-done.9) | copy-start | bytes 6291460
  1019.4 13.0 %copy-start.12 = (f32[16,4,8,8,64]{4,3,2,1,0:T(8,128)S(1)}, f32[16,4,8,8,64]{4,3,2,1,0:T(8,128)}, u32[]{:S(2)}) copy-start(f32[16,4,8,8,64]{4,3,2,1,0:T(8,128)} %copy-done.11) | copy-start | bytes 3145732
  1019.4 13.0 %copy-start.14 = (f32[16,4,8,8,64]{4,3,2,1,0:T(8,128)S(1)}, f32[16,4,8,8,64]{4,3,2,1,0:T(8,128)}, u32[]{:S(2)}) copy-start(f32[16,4,8,8,64]{4,3,2,1,0:T(8,128)} %copy-done.13) | copy-start | bytes 3145732
  1019.4 13.0 %copy-start.19 = (f32[8,1,4,128,192]{4,3,2,0,1:T(8,128)S(1)}, f32[8,1,4,128,192]{4,3,2,0,1:T(8,128)}, u32[]{:S(2)}) copy-start(f32[8,1,4,128,192]{4,3,2,0,1:T(8,128)} %copy.348) | copy-start | bytes 9437188
  1019.4 13.0 %copy-start.20 = (f32[8,1,4,128,192]{4,3,2,0,1:T(8,128)S(1)}, f32[8,1,4,128,192]{4,3,2,0,1:T(8,128)}, u32[]{:S(2)}) copy-start(f32[8,1,4,128,192]{4,3,2,0,1:T(8,128)} %copy.350) | copy-start | bytes 9437188
  1032.4 6.9 copy-start.39
  1042.7 4.6 copy-start.42
  1053.2 24.0 %all-to-all-start.3 = ((f32[2,128,2,8,96]{1,4,3,2,0:T(8,128)}), f32[2,128,2,8,96]{1,4,3,2,0:T(8,128)S(1)}, u32[]{:S(2)}, u32[]{:S(2)}) async-start(f32[2,128,2,8,96]{1,4,3,2,0:T(8,128)} %copy.375), calls=%async_computation.3 | async-start | bytes 3145728 | tf_op jit(solution)/shard_map/all_to_all | solution.py:132
  1077.2 28.7 %all-to-all-start.9 = ((f32[16,8,2,8,96]{4,3,2,1,0:T(8,128)}), f32[16,8,2,8,96]{4,3,2,1,0:T(8,128)S(1)}, u32[]{:S(2)}, u32[]{:S(2)}) async-start(f32[16,8,2,8,96]{4,3,2,1,0:T(8,128)} %bitcast.208), calls=%async_computation.9 | async-start | bytes 2097152 | tf_op jit(solution)/shard_map/all_to_all | solution.py:134
  1105.9 1.0 copy-start.40
  1106.8 29.9 %all-to-all-start.4 = ((f32[16,8,2,8,96]{4,3,2,1,0:T(8,128)}), f32[16,8,2,8,96]{4,3,2,1,0:T(8,128)}, u32[]{:S(2)}, u32[]{:S(2)}) async-start(f32[16,8,2,8,96]{4,3,2,1,0:T(8,128)} %bitcast.93), calls=%async_computation.4 | async-start | bytes 2097152 | tf_op jit(solution)/shard_map/all_to_all | solution.py:134
  1115.1 25.5 %copy-start.21 = (f32[2,1,8,96,256]{4,3,2,1,0:T(8,128)S(1)}, f32[2,1,8,96,256]{4,3,2,1,0:T(8,128)}, u32[]{:S(2)}) copy-start(f32[2,1,8,96,256]{4,3,2,1,0:T(8,128)} %param.11) | copy-start | bytes 4718596
Sparse Core Ops, SparseCore 0:
  380.7 294.9 all-gather.1
